TPU v7x, 32 devices: a whole 2x2x4 slice. The times are simulated.
32 devices in a mesh: blk: 8 (over z, y), vec: 4 (over x, core).
Axes of the slice: x: 2, y: 2, z: 4, core: 2. Of those that a mesh axis runs over, the one named last changes fastest.
Arguments:
- cholesky_factors: bfloat16 [384, 128, 1024], P(('blk', 'vec')), may hold values from -0.1875 to 0.1875
- walker_green: bfloat16 [8, 128, 1024], P('blk'), may hold values from -8 to 8
Outputs:
- exchange_grad: float32 [8, 128, 1024], P('blk', None, 'vec')
- exchange_energy: float32 [8], P('blk')
All inputs are finite; a program needn't handle non-finite values.
Results may differ from a plain program's by a relative error of at most 0.0029.
Values may be sent and summed in bfloat16 or wider, within the bound.
A program may use at most 64 MiB of HBM per device.

v0:
```python
import functools
import math

import jax
import jax.numpy as jnp
from jax import lax
from jax.experimental import pallas as pl
from jax.experimental.pallas import tpu as pltpu
from jax.sharding import PartitionSpec as P

MESH = pl.DeviceIdType.MESH


def flip(value, step, size):
    total, bit = 0, 1
    while bit < size:
        total = total + ((value // bit + step // bit) % 2) * bit
        bit *= 2
    return total


def kernel(
    groups, vec_count, energy_scale, grad_scale,
    l_hbm, g_hbm,
    grad_ref, energy_ref,
    l_ref, green, gall, inter, prod, core_out, core_in, a1_out, a1_in, b1_out, b1_in, own, a2_out, a2_in, b2_out, b2_in, kept, z_out, z_in, ebuf, e_in,
    l_sem, g_sem,
    gz_s, gz_r, gx_s, gx_r, gc0_s, gc0_r, gc1_s, gc1_r, rz_s, rz_r,
    gy_s, gy_r, rc_s, rc_r, rx_s, rx_r, ry_s, ry_r, e_s, e_r,
):
    blk, vec = lax.axis_index("blk"), lax.axis_index("vec")
    z, y = blk // 2, blk % 2
    x, c = vec // 2, vec % 2
    el = g_hbm.shape[1]
    norb = g_hbm.shape[2]
    vectors = l_hbm.shape[0]
    quarter = norb // vec_count
    half = norb // 2

    core_peer = {"blk": blk, "vec": x * 2 + (1 - c)}
    x_peer = {"blk": blk, "vec": (1 - x) * 2 + c}
    y_peer = {"blk": z * 2 + (1 - y), "vec": vec}

    def z_peer(k):
        return {"blk": flip(z, k, groups) * 2 + y, "vec": vec}

    def home(k, j):
        return {"blk": flip(z, k, groups) * 2 + y, "vec": flip(vec, j, vec_count)}

    mine = pl.ds(pl.multiple_of(c * half, half), half)
    part_me = pl.ds(pl.multiple_of(c * half + x * quarter, quarter), quarter)
    part_other = pl.ds(pl.multiple_of(c * half + (1 - x) * quarter, quarter), quarter)
    rows_me = pl.ds(pl.multiple_of(y * el, el), el)
    rows_other = pl.ds(pl.multiple_of((1 - y) * el, el), el)

    def remote(src, dst, s, r, peer):
        return pltpu.make_async_remote_copy(
            src_ref=src, dst_ref=dst, send_sem=s, recv_sem=r, device_id=peer, device_id_type=MESH
        )

    def gz(k):
        return remote(
            gall.at[0, y, part_me], gall.at[k, y, part_me], gz_s.at[k], gz_r.at[k], z_peer(k)
        )

    def gx(k):
        return remote(
            gall.at[k, y, part_me], gall.at[k, y, part_me], gx_s.at[k], gx_r.at[k], x_peer
        )

    def gy_first():
        return remote(
            gall.at[0, y, mine], gall.at[0, y, mine], gy_s.at[0, 0], gy_r.at[0, 0], y_peer
        )

    def gy(k, n):
        part = (part_me, part_other)[n]
        return remote(
            gall.at[k, y, part], gall.at[k, y, part], gy_s.at[k, n], gy_r.at[k, n], y_peer
        )

    def gx_other(k):
        view = gall.at[k, 1 - y, part_me]
        return remote(view, view, gy_s.at[k, 1], gy_r.at[k, 1], x_peer)

    def gc0(k):
        return remote(
            gall.at[k, y, mine], gall.at[k, y, mine], gc0_s.at[k], gc0_r.at[k], core_peer
        )

    def gc1(k):
        return remote(
            gall.at[k, 1 - y, mine], gall.at[k, 1 - y, mine], gc1_s.at[k], gc1_r.at[k], core_peer
        )

    def rc(k, part):
        return remote(
            core_out.at[k, part], core_in.at[k, part], rc_s.at[k, part], rc_r.at[k, part], core_peer
        )

    def rx(k, n):
        out, into = ((a1_out, a1_in), (b2_out, b2_in))[n]
        return remote(out.at[k], into.at[k], rx_s.at[k, n], rx_r.at[k, n], x_peer)

    def ry(k, n):
        out, into = ((b1_out, b1_in), (a2_out, a2_in))[n]
        return remote(out.at[k], into.at[k], ry_s.at[k, n], ry_r.at[k, n], y_peer)

    def rz(k):
        return remote(z_out.at[k], z_in.at[k], rz_s.at[k], rz_r.at[k], z_peer(k))

    def energy_send(k, j):
        return remote(
            ebuf.at[k, vec], e_in.at[k, vec], e_s.at[k, j], e_r.at[k, j], home(k, j)
        )

    l_copy = pltpu.make_async_copy(l_hbm, l_ref, l_sem)
    g_copy = pltpu.make_async_copy(g_hbm.at[0], green, g_sem)
    g_copy.start()
    l_copy.start()

    barrier = pltpu.get_barrier_semaphore()
    pl.semaphore_signal(barrier, inc=1, device_id=y_peer, device_id_type=MESH)
    for k in range(groups):
        for j in range(vec_count):
            if k + j > 0:
                pl.semaphore_signal(barrier, inc=1, device_id=home(k, j), device_id_type=MESH)
    g_copy.wait()
    gall[0, y] = green[...].T
    pl.semaphore_wait(barrier, groups * vec_count)

    for k in range(1, groups):
        gz(k).start()

    def first_service(k):
        gz(k).wait_recv()
        gx(k).start()
        gy(k, 0).start()

    def second_service(k, odd):
        gx(k).wait_recv()
        gc0(k).start()
        if odd:
            gy(k, 0).wait_recv()
            gx_other(k).start()
        else:
            gy(k, 1).start()

    def third_service(k, odd):
        if odd:
            gx_other(k).wait_recv()
        else:
            gy(k, 0).wait_recv()
            gy(k, 1).wait_recv()
        gc1(k).start()

    first_service(1)
    if groups > 2:
        first_service(2)
    gy_first().start()
    second_service(1, True)
    if groups > 2:
        second_service(2, False)
        first_service(3)
    third_service(1, True)
    if groups > 2:
        third_service(2, False)
    gy_first().wait_recv()
    gc1(0).start()
    l_copy.wait()

    def columns(xq, cq):
        return pl.ds(pl.multiple_of((xq * 2 + cq) * quarter, quarter), quarter)

    def product(xq):
        cols = pl.ds(pl.multiple_of(xq * half, half), half)
        prod[...] = jnp.dot(
            inter[...],
            l_ref[:, :, cols].reshape(vectors * el, half),
            preferred_element_type=jnp.float32,
        )

    def prod_part(h, cq):
        return prod[
            h * 2 * el : (h + 1) * 2 * el, pl.ds(pl.multiple_of(cq * quarter, quarter), quarter)
        ]

    f32, bf = jnp.float32, jnp.bfloat16
    hq = quarter // 2

    def y_stage(k):
        rx(k, 0).wait_recv()
        a2_out[k] = (own[k, 1, rows_other, :hq] + a1_in[k, rows_other].astype(f32)).astype(bf)
        ry(k, 1).start()
        ry(k, 0).wait_recv()
        b2_out[k] = (own[k, 0, rows_me, hq:] + b1_in[k, 0].astype(f32)).astype(bf)
        rx(k, 1).start()
        kept[k, :, :hq] = own[k, 1, rows_me, :hq] + a1_in[k, rows_me].astype(f32)
        kept[k, :, hq:] = own[k, 1, rows_me, hq:] + b1_in[k, 1].astype(f32)

    def z_stage(k):
        ry(k, 1).wait_recv()
        kept[k, :, :hq] += a2_in[k].astype(f32)
        rx(k, 1).wait_recv()
        kept[k, :, hq:] += b2_in[k].astype(f32)

        @pl.when(k > 0)
        def _():
            z_out[k] = kept[k].astype(jnp.bfloat16)
            rz(k).start()

        energy = jnp.sum(kept[k] * gall[k, y, columns(x, c)].astype(jnp.float32).T)
        ebuf[k, vec] = jnp.full(ebuf.shape[2:], energy, jnp.float32)
        for j in range(1, vec_count):
            energy_send(k, j).start()

        @pl.when(k > 0)
        def _():
            energy_send(k, 0).start()

    chunk = vectors

    def step(pair, carry):
        base = 2 * pair
        more = base + 2 < groups
        after = base + 4 < groups
        ks = (base + 1, lax.rem(base + 2, groups))
        for k in ks:
            gc1(k).wait_recv()
        gc0(ks[0]).wait_recv()

        @pl.when(more)
        def _():
            gc0(ks[1]).wait_recv()
            second_service(base + 3, True)

        @pl.when(after)
        def _():
            first_service(base + 4)

        for first in range(0, vectors, chunk):
            block = lax.dot_general(
                l_ref[first : first + chunk].reshape(chunk * el, norb),
                jnp.concatenate([gall[ks[w // 2], w % 2] for w in range(4)], axis=1),
                (((1,), (0,)), ((), ())),
                preferred_element_type=jnp.float32,
            ).astype(jnp.bfloat16)
            for g in range(chunk):
                for w in range(4):
                    inter[w * el : (w + 1) * el, (first + g) * el : (first + g + 1) * el] = block[
                        g * el : (g + 1) * el, w * el : (w + 1) * el
                    ]

        for h in range(2):

            @pl.when(pair > 0)
            def _():
                y_stage(base + h - 1)

        product(1 - x)
        for h in range(2):
            k = ks[h]
            core_out[k, 0] = prod_part(h, 1 - c).astype(bf)
            rc(k, 0).start()
            own[k, 0] = prod_part(h, c)

        @pl.when(more)
        def _():
            third_service(base + 3, True)

        @pl.when(after)
        def _():
            second_service(base + 4, False)

        product(x)
        for h in range(2):
            k = ks[h]
            core_out[k, 1] = prod_part(h, 1 - c).astype(bf)
            rc(k, 1).start()
        for h in range(2):
            k = ks[h]
            rc(k, 0).wait_recv()
            own[k, 0] += core_in[k, 0].astype(f32)
            a1_out[k] = own[k, 0, :, :hq].astype(bf)
            rx(k, 0).start()
        for h in range(2):
            k = ks[h]
            rc(k, 1).wait_recv()
            own[k, 1] = prod_part(h, c) + core_in[k, 1].astype(f32)
            for n in range(2):
                b1_out[k, n] = own[k, n, rows_other, hq:].astype(bf)
            ry(k, 0).start()

        @pl.when(after)
        def _():
            third_service(base + 4, False)
            first_service(base + 5)

        @pl.when(pair > 0)
        def _():
            z_stage(base - 1)
            z_stage(base)

        return carry

    lax.fori_loop(0, groups // 2, step, 0)
    last = groups - 1
    y_stage(last)
    y_stage(0)
    z_stage(last)
    z_stage(0)

    total = kept[0]
    for k in range(1, groups):
        rz(k).wait_recv()
        total = total + z_in[k].astype(jnp.float32)
    grad_ref[...] = total * grad_scale

    e_in[0, vec] = ebuf[0, vec]
    for k in range(groups):
        for j in range(vec_count):
            if k + j > 0:
                energy_send(k, j).wait_recv()
    energies = jnp.zeros(e_in.shape[2:], jnp.float32)
    for k in range(groups):
        for n in range(vec_count):
            energies = energies + e_in[k, n]
    energy_ref[0] = jnp.max(energies) * energy_scale

    gy_first().wait_send()
    gc1(0).wait_send()
    for k in range(groups):
        for n in range(2):
            rc(k, n).wait_send()
            rx(k, n).wait_send()
            ry(k, n).wait_send()
        for j in range(vec_count):
            if k + j > 0:
                energy_send(k, j).wait_send()
        if k > 0:
            gz(k).wait_send()
            gx(k).wait_send()
            gy(k, 0).wait_send()
            (gx_other(k) if k % 2 else gy(k, 1)).wait_send()
            gc0(k).wait_send()
            gc1(k).wait_send()
            rz(k).wait_send()


def shards(cholesky_factors, walker_green):
    blk_count = lax.axis_size("blk")
    vec_count = lax.axis_size("vec")
    vectors, el, norb = cholesky_factors.shape
    vector_total = vectors * blk_count * vec_count
    groups = blk_count // 2
    assert vec_count == 4 and groups > 1 and groups & (groups - 1) == 0
    quarter = norb // vec_count
    hq = quarter // 2
    bf, f32 = jnp.bfloat16, jnp.float32
    dma = pltpu.SemaphoreType.DMA
    flops = 4 * blk_count * vectors * el * el * norb
    gradient, energy = pl.pallas_call(
        functools.partial(
            kernel, groups, vec_count, -0.5 / (el * vector_total), 1.0 / math.sqrt(vector_total)
        ),
        out_shape=(
            jax.ShapeDtypeStruct((el, quarter), f32),
            jax.ShapeDtypeStruct((1,), f32),
        ),
        in_specs=[pl.BlockSpec(memory_space=pl.ANY)] * 2,
        out_specs=(
            pl.BlockSpec(memory_space=pltpu.VMEM),
            pl.BlockSpec(memory_space=pltpu.SMEM),
        ),
        scratch_shapes=[
            pltpu.VMEM((vectors, el, norb), bf),
            pltpu.VMEM((el, norb), bf),
            pltpu.VMEM((groups, 2, norb, el), bf),
            pltpu.VMEM((4 * el, vectors * el), bf),
            pltpu.VMEM((4 * el, norb // 2), f32),
            pltpu.VMEM((groups, 2, 2 * el, quarter), bf),
            pltpu.VMEM((groups, 2, 2 * el, quarter), bf),
            pltpu.VMEM((groups, 2 * el, hq), bf),
            pltpu.VMEM((groups, 2 * el, hq), bf),
            pltpu.VMEM((groups, 2, el, hq), bf),
            pltpu.VMEM((groups, 2, el, hq), bf),
            pltpu.VMEM((groups, 2, 2 * el, quarter), f32),
            pltpu.VMEM((groups, el, hq), bf),
            pltpu.VMEM((groups, el, hq), bf),
            pltpu.VMEM((groups, el, hq), bf),
            pltpu.VMEM((groups, el, hq), bf),
            pltpu.VMEM((groups, el, quarter), f32),
            pltpu.VMEM((groups, el, quarter), bf),
            pltpu.VMEM((groups, el, quarter), bf),
            pltpu.VMEM((groups, vec_count, 8, 128), f32),
            pltpu.VMEM((groups, vec_count, 8, 128), f32),
            dma, dma,
        ]
        + [dma((groups,))] * 10
        + [dma((groups, 2))] * 8
        + [dma((groups, vec_count))] * 2,
        compiler_params=pltpu.CompilerParams(
            collective_id=0, has_side_effects=True, vmem_limit_bytes=56 * 1024 * 1024
        ),
        cost_estimate=pl.CostEstimate(
            flops=flops, bytes_accessed=2 * vectors * el * norb, transcendentals=0
        ),
        name="exchange",
    )(cholesky_factors, walker_green)
    return gradient[None], energy


def solution(mesh):
    return jax.shard_map(
        shards,
        mesh=mesh,
        in_specs=(P(("blk", "vec"), None, None), P("blk", None, None)),
        out_specs=(P("blk", None, "vec"), P("blk")),
        check_vma=False,
    )
```

profile of v0, /device:TPU:0, one launch (start us, length us, event | category | flops | bytes accessed | tf_op | source)
XLA Modules:
  0.0 52.0 jit_solution(10408382915180986094)
XLA Ops:
  0.6 47.9 %exchange.1 = (f32[128,256]{1,0:T(8,128)}, f32[1]{0:T(128)}) custom-call(bf16[12,128,1024]{2,1,0:T(8,128)(2,1)} %l_hbm.1, bf16[1,128,1024]{2,1,0:T(8,128)(2,1)} %g_hbm.1), custom_call_target="tpu_custom_call" | custom-call | flops 6442450944 | bytes 3145728 | tf_op jit(solution)/shard_map/exchange/pallas_call | solution.py:362
  48.6 1.6 %copy.6 = f32[1,128,256]{2,1,0:T(8,128)} copy(f32[1,128,256]{2,1,0:T(8,128)} %bitcast.1) | data formatting | bytes 262144
where the time goes:
time: 52.1 us; the launch traced here: 52 us
  Pallas kernels  47.9 us (92%)
  between operations  2.45 us (5%)
  local copies, waits for them, and re-layouts  1.57 us (3%)
    pallas_call x1, Pallas kernels, shards(): pl.pallas_call(functools.partial(kernel, groups, vec_count, -0.5 / (el *...  47.9 us
    unnamed x1, local copies, waits for them, and re-layouts  1.57 us

commit v1 on v0

--- a/solution.py
+++ b/solution.py
@@ -163,10 +163,6 @@
         second_service(2, False)
         first_service(3)
     third_service(1, True)
-    if groups > 2:
-        third_service(2, False)
-    gy_first().wait_recv()
-    gc1(0).start()
     l_copy.wait()
 
     def columns(xq, cq):
@@ -180,10 +176,16 @@
             preferred_element_type=jnp.float32,
         )
 
-    def prod_part(h, cq):
-        return prod[
-            h * 2 * el : (h + 1) * 2 * el, pl.ds(pl.multiple_of(cq * quarter, quarter), quarter)
-        ]
+    def prod_part(cq):
+        return prod[:, pl.ds(pl.multiple_of(cq * quarter, quarter), quarter)]
+
+    def serve(service, k):
+        for odd in (True, False):
+
+            @pl.when((k < groups) & (lax.rem(k, 2) == int(odd)))
+            def _():
+                service(k, odd)
+
 
     f32, bf = jnp.float32, jnp.bfloat16
     hq = quarter // 2
@@ -220,94 +222,68 @@
 
     chunk = vectors
 
-    def step(pair, carry):
-        base = 2 * pair
-        more = base + 2 < groups
-        after = base + 4 < groups
-        ks = (base + 1, lax.rem(base + 2, groups))
-        for k in ks:
-            gc1(k).wait_recv()
-        gc0(ks[0]).wait_recv()
-
-        @pl.when(more)
-        def _():
-            gc0(ks[1]).wait_recv()
-            second_service(base + 3, True)
-
-        @pl.when(after)
-        def _():
-            first_service(base + 4)
+    def step(s, carry):
+        k = lax.rem(s + 1, groups)
+        gc1(k).wait_recv()
+
+        @pl.when(k > 0)
+        def _():
+            gc0(k).wait_recv()
 
         for first in range(0, vectors, chunk):
             block = lax.dot_general(
                 l_ref[first : first + chunk].reshape(chunk * el, norb),
-                jnp.concatenate([gall[ks[w // 2], w % 2] for w in range(4)], axis=1),
+                jnp.concatenate([gall[k, 0], gall[k, 1]], axis=1),
                 (((1,), (0,)), ((), ())),
                 preferred_element_type=jnp.float32,
             ).astype(jnp.bfloat16)
             for g in range(chunk):
-                for w in range(4):
+                for w in range(2):
                     inter[w * el : (w + 1) * el, (first + g) * el : (first + g + 1) * el] = block[
                         g * el : (g + 1) * el, w * el : (w + 1) * el
                     ]
 
-        for h in range(2):
-
-            @pl.when(pair > 0)
-            def _():
-                y_stage(base + h - 1)
+        serve(third_service, s + 2)
+        serve(second_service, s + 3)
+
+        @pl.when(s > 0)
+        def _():
+            y_stage(s)
 
         product(1 - x)
-        for h in range(2):
-            k = ks[h]
-            core_out[k, 0] = prod_part(h, 1 - c).astype(bf)
-            rc(k, 0).start()
-            own[k, 0] = prod_part(h, c)
-
-        @pl.when(more)
-        def _():
-            third_service(base + 3, True)
-
-        @pl.when(after)
-        def _():
-            second_service(base + 4, False)
-
+        core_out[k, 0] = prod_part(1 - c).astype(bf)
+        rc(k, 0).start()
+        own[k, 0] = prod_part(c)
         product(x)
-        for h in range(2):
-            k = ks[h]
-            core_out[k, 1] = prod_part(h, 1 - c).astype(bf)
-            rc(k, 1).start()
-        for h in range(2):
-            k = ks[h]
-            rc(k, 0).wait_recv()
-            own[k, 0] += core_in[k, 0].astype(f32)
-            a1_out[k] = own[k, 0, :, :hq].astype(bf)
-            rx(k, 0).start()
-        for h in range(2):
-            k = ks[h]
-            rc(k, 1).wait_recv()
-            own[k, 1] = prod_part(h, c) + core_in[k, 1].astype(f32)
-            for n in range(2):
-                b1_out[k, n] = own[k, n, rows_other, hq:].astype(bf)
-            ry(k, 0).start()
-
-        @pl.when(after)
-        def _():
-            third_service(base + 4, False)
-            first_service(base + 5)
-
-        @pl.when(pair > 0)
-        def _():
-            z_stage(base - 1)
-            z_stage(base)
+        core_out[k, 1] = prod_part(1 - c).astype(bf)
+        rc(k, 1).start()
+        rc(k, 0).wait_recv()
+        own[k, 0] += core_in[k, 0].astype(f32)
+        a1_out[k] = own[k, 0, :, :hq].astype(bf)
+        rx(k, 0).start()
+        rc(k, 1).wait_recv()
+        own[k, 1] = prod_part(c) + core_in[k, 1].astype(f32)
+        for n in range(2):
+            b1_out[k, n] = own[k, n, rows_other, hq:].astype(bf)
+        ry(k, 0).start()
+
+        @pl.when(s + 4 < groups)
+        def _():
+            first_service(s + 4)
+
+        @pl.when(s == 0)
+        def _():
+            gy_first().wait_recv()
+            gc1(0).start()
+
+        @pl.when(s > 0)
+        def _():
+            z_stage(s)
 
         return carry
 
-    lax.fori_loop(0, groups // 2, step, 0)
-    last = groups - 1
-    y_stage(last)
+    lax.fori_loop(0, groups, step, 0)
     y_stage(0)
-    z_stage(last)
     z_stage(0)
 
     total = kept[0]
@@ -376,8 +352,8 @@
             pltpu.VMEM((vectors, el, norb), bf),
             pltpu.VMEM((el, norb), bf),
             pltpu.VMEM((groups, 2, norb, el), bf),
-            pltpu.VMEM((4 * el, vectors * el), bf),
-            pltpu.VMEM((4 * el, norb // 2), f32),
+            pltpu.VMEM((2 * el, vectors * el), bf),
+            pltpu.VMEM((2 * el, norb // 2), f32),
             pltpu.VMEM((groups, 2, 2 * el, quarter), bf),
             pltpu.VMEM((groups, 2, 2 * el, quarter), bf),
             pltpu.VMEM((groups, 2 * el, hq), bf),

time: 52.1 us -> 60.3 us (1.16)
  Pallas kernels: 47.9 us -> 56.1 us
    pallas_call x1, Pallas kernels: 47.9 us -> 56.1 us  [shards(): pl.pallas_call(functools.partial(kernel, groups, vec_count, -0.5 / (el *...]
where the time goes in v1:
time: 60.3 us; the launch traced here: 60.1 us
  Pallas kernels  56.1 us (93%)
  between operations  2.45 us (4%)
  local copies, waits for them, and re-layouts  1.57 us (3%)
    pallas_call x1, Pallas kernels, shards(): pl.pallas_call(functools.partial(kernel, groups, vec_count, -0.5 / (el *...  56.1 us
    unnamed x1, local copies, waits for them, and re-layouts  1.57 us

profile of v1, /device:TPU:0, one launch (start us, length us, event | category | flops | bytes accessed | tf_op | source)
XLA Modules:
  0.0 60.1 jit_solution(9867302975295451866)
XLA Ops:
  0.6 56.1 %exchange.1 = (f32[128,256]{1,0:T(8,128)}, f32[1]{0:T(128)}) custom-call(bf16[12,128,1024]{2,1,0:T(8,128)(2,1)} %l_hbm.1, bf16[1,128,1024]{2,1,0:T(8,128)(2,1)} %g_hbm.1), custom_call_target="tpu_custom_call" | custom-call | flops 6442450944 | bytes 3145728 | tf_op jit(solution)/shard_map/exchange/pallas_call | solution.py:338
  56.7 1.6 %copy.6 = f32[1,128,256]{2,1,0:T(8,128)} copy(f32[1,128,256]{2,1,0:T(8,128)} %bitcast.1) | data formatting | bytes 262144
